TPU v7x, 512 devices: a whole 4x8x8 slice. The times are simulated.
512 devices in a mesh: dom: 64 (over x, z, core), col: 8 (over y).
Axes of the slice: x: 4, y: 8, z: 8, core: 2. Of those that a mesh axis runs over, the one named last changes fastest.
Arguments:
- snapshots: bfloat16 [128, 3, 131072], P('col', None, 'dom'), may hold values from -30 to 30
- mass_tiles: bfloat16 [16, 3, 3, 131072], P(None, None, None, 'dom'), may hold values from -2 to 2
- tile_slot: int32 [15, 131072], P(None, 'dom'), may hold values from 0 to 3071
- send_up: int32 [32768], P('dom'), may hold values from 0 to 2047
- send_down: int32 [32768], P('dom'), may hold values from 0 to 2047
Outputs:
- mass_snap: bfloat16 [128, 3, 131072], P('col', None, 'dom')
- gram: float32 [128, 128], P(None, 'col')
Inputs may be any that keep to these rules, and one draw needn't show every extreme that they name: `tile_slot`: slots below 2048 are the partition's own nodes, the next 512 those received from the previous partition, the last 512 those from the next partition.
All inputs are finite; a program needn't handle non-finite values.
Results may differ from a plain program's by a relative error of at most 0.001.
Values may be sent and summed in bfloat16 or wider, within the bound.
A program may use at most 64 MiB of HBM per device.

v0:
```python
import jax
import jax.numpy as jnp
from jax import lax
from jax.sharding import PartitionSpec as P


def shifted(value, axis, steps):
    count = lax.axis_size(axis)
    leading, last = (max(0, -steps), min(count, count - steps))
    return lax.ppermute(value, axis, [(source, source + steps) for source in range(leading, last)])


def couple(tiles, values):
    total_sum = tiles[None, :, 0, :].astype(jnp.float32) * values[:, None, 0, :].astype(jnp.float32)
    for in_comp in (1, 2):
        total_sum = total_sum + tiles[None, :, in_comp, :].astype(jnp.float32) * values[
            :, None, in_comp, :
        ].astype(jnp.float32)
    return total_sum


def apply_mass(local_snap, flat_ext, mass_tiles, tile_slot):
    snap_count = local_snap.shape[0]
    node_count = local_snap.shape[2]
    others = tile_slot.shape[0]
    total_sum = couple(mass_tiles[0], local_snap)
    gathered = jnp.take(flat_ext, tile_slot.reshape(-1), axis=1)
    gathered = gathered.reshape(snap_count, 3, others, node_count)
    for in_comp in (0, 1, 2):
        tile_part = jnp.transpose(mass_tiles[1:, :, in_comp, :], (1, 0, 2)).astype(jnp.float32)
        values = gathered[:, in_comp].astype(jnp.float32)
        total_sum = total_sum + jnp.sum(tile_part[None] * values[:, None], axis=2)
    return total_sum.astype(jnp.bfloat16)


def inner_products(left_rows, right_rows):
    left_flat = left_rows.reshape(left_rows.shape[0], -1)
    right_flat = right_rows.reshape(right_rows.shape[0], -1)
    return lax.dot_general(
        left_flat, right_flat, (((1,), (1,)), ((), ())), preferred_element_type=jnp.float32
    )


def body(snapshots, mass_tiles, tile_slot, send_up, send_down):
    snap_count = snapshots.shape[0]
    flat_local = snapshots.reshape(snap_count * 3, -1)
    to_upper = jnp.take(flat_local, send_up, axis=1)
    to_lower = jnp.take(flat_local, send_down, axis=1)
    from_lower = shifted(to_upper, "dom", 1)
    from_upper = shifted(to_lower, "dom", -1)
    flat_ext = jnp.concatenate([flat_local, from_lower, from_upper], axis=1)
    mass_snap = apply_mass(snapshots, flat_ext, mass_tiles, tile_slot)
    block_terms = inner_products(lax.all_gather(snapshots, "col", axis=0, tiled=True), mass_snap)
    summed_gram = lax.psum(block_terms, "dom")
    node_total = 3.0 * snapshots.shape[2] * lax.axis_size("dom")
    gram = summed_gram / node_total
    return (mass_snap, gram)


def solution(mesh):
    placed = (P("col", None, "dom"), P(None, None, None, "dom"), P(None, "dom"), P("dom"), P("dom"))
    return jax.shard_map(
        body,
        mesh=mesh,
        in_specs=placed,
        out_specs=(P("col", None, "dom"), P(None, "col")),
        check_vma=False,
    )
```

profile of v0, /device:TPU:1, one launch (start us, length us, event | category | flops | bytes accessed | tf_op | source)
XLA Modules:
  0.0 294.7 jit_solution(7028751788480375914)
XLA Ops:
  7.2 0.0 copy-start
  7.2 0.0 copy-start.4
  7.2 0.0 copy-start.8
  7.2 0.0 all-gather.2.cloned.1.call-start
  7.2 0.7 all-gather.2.cloned.1.call-update
  7.9 1.1 copy.43
  9.0 0.7 compare_select_fusion.3
  9.7 0.7 compare_and_fusion.2
  10.4 0.2 reshape.93
  10.6 0.3 copy.46
  10.9 1.3 gather_fusion.1
  12.2 0.1 select_bitcast_fusion.1
  12.4 5.4 %collective-permute-start = (bf16[48,512]{0,1:T(8,128)(2,1)S(1)}, bf16[48,512]{0,1:T(8,128)(2,1)S(1)}, u32[]{:S(2)}, u32[]{:S(2)}) collective-permute-start(bf16[48,512]{0,1:T(8,128)(2,1)S(1)} %select_bitcast_fusion.1), channel_id=1, source_target_pairs={{0,8},{8,16},{16,24},{24,32},{32,40},{40,48},{48,56},{56,64},{64,7... | collective-permute-start | bytes 147464 | tf_op jit(solution)/shard_map/ppermute | solution.py:10
  17.8 0.7 compare_select_fusion.2
  18.4 0.7 compare_and_fusion.1
  19.1 1.3 gather_fusion.2
  20.5 0.1 select_bitcast_fusion
  20.6 4.7 %collective-permute-start.1 = (bf16[48,512]{0,1:T(8,128)(2,1)S(1)}, bf16[48,512]{0,1:T(8,128)(2,1)S(1)}, u32[]{:S(2)}, u32[]{:S(2)}) collective-permute-start(bf16[48,512]{0,1:T(8,128)(2,1)S(1)} %select_bitcast_fusion), channel_id=1, source_target_pairs={{8,0},{16,8},{24,16},{32,24},{40,32},{48,40},{56,48},{64,56},{72,6... | collective-permute-start | bytes 147464 | tf_op jit(solution)/shard_map/ppermute | solution.py:10
  25.3 0.0 copy-done.4
  25.3 1.1 convert_bitcast_fusion.2
  26.5 0.0 copy-done
  26.5 0.7 bitcast_convert_fusion.2
  27.2 0.0 copy-done.8
  27.2 0.6 compare_and_fusion
  27.9 0.1 copy.53
  28.0 0.1 compare_select_fusion
  28.2 0.1 slice_convert_fusion.2
  28.3 0.6 copy_bitcast_fusion.1
  28.9 0.6 copy.60
  29.6 0.0 collective-permute-done
  29.6 0.0 collective-permute-done.1
  29.6 0.2 pad_maximum_fusion
  29.7 107.0 %gather_fusion = bf16[30720,48]{1,0:T(8,128)(2,1)} fusion(bf16[48,3072]{0,1:T(8,128)(2,1)S(1)} %pad_maximum_fusion, s32[30720]{0:T(1024)S(1)} %broadcast_clamp_fusion), kind=kCustom, calls=%fused_computation.2 | custom fusion | bytes 6021120 | tf_op jit(solution)/shard_map/jit(_take)/gather | solution.py:27
  136.8 8.1 %copy.47 = bf16[48,30720]{1,0:T(8,128)(2,1)} copy(bf16[48,30720]{0,1:T(8,128)(2,1)} %bitcast.65) | data formatting | bytes 5898240 | tf_op jit(solution)/shard_map/jit(_take)/gather | solution.py:27
  144.9 4.4 %gather.10 = bf16[16,3,15,2048]{3,2,1,0:T(8,128)(2,1)S(1)} reshape(bf16[48,30720]{1,0:T(8,128)(2,1)} %copy.47) | data formatting | bytes 5898240 | tf_op jit(solution)/shard_map/jit(_take)/gather | solution.py:27
  149.3 4.3 %copy_select_fusion = bf16[16,3,15,2048]{3,0,2,1:T(8,128)(2,1)S(1)} fusion(bf16[16,3,15,2048]{3,2,1,0:T(8,128)(2,1)S(1)} %gather.10, pred[15,2048]{1,0:T(8,128)(4,1)} %compare_and_fusion), kind=kLoop, calls=%fused_computation.6 | loop fusion | flops 1474560 | bytes 5928960 | tf_op jit(solution)/shard_map/jit(_take)/select_n | solution.py:27
  153.6 0.6 fusion.2
  154.2 0.0 copy-start.1
  154.2 0.0 copy-start.2
  154.2 0.4 multiply_reduce_fusion.2
  154.7 0.0 copy-start.5
  154.7 0.0 copy-start.6
  154.7 0.0 copy-start.7
  154.7 0.0 copy-start.9
  154.7 0.0 copy-start.10
  154.7 0.0 copy-start.11
  154.7 0.5 copy-done.1
  155.2 0.1 copy-done.2
  155.3 1.0 multiply_reduce_fusion
  156.3 0.0 copy-done.5
  156.3 0.0 copy-done.6
  156.4 0.0 copy-done.7
  156.4 0.0 copy-done.9
  156.4 0.0 copy-done.10
  156.4 0.0 copy-done.11
  156.4 0.1 add_convert_fusion
  156.5 0.0 copy-start.3
  156.5 0.0 all-gather.2.cloned.1.call-done
  156.6 2.0 convolution_bitcast_fusion
  158.5 128.7 %psum.7 = f32[128,16]{0,1:T(8,128)S(1)} all-reduce(f32[128,16]{0,1:T(8,128)S(1)} %convolution_bitcast_fusion), channel_id=1, replica_groups=mesh['dom'=64,'col'=8] {'dom'}, use_global_device_ids=true, to_apply=%region_3.5 | all-reduce | flops 2048 | bytes 16384 | tf_op jit(solution)/shard_map/psum | solution.py:54
  287.2 0.6 broadcast_multiply_fusion
  287.8 0.0 copy-done.3
  (5 shorter events, 0.1 us)
Async XLA Ops:
  7.2 19.3 %copy-start = (bf16[16,3,2048]{2,0,1:T(8,128)(2,1)S(1)}, bf16[16,3,2048]{2,0,1:T(8,128)(2,1)}, u32[]{:S(2)}) copy-start(bf16[16,3,2048]{2,0,1:T(8,128)(2,1)} %param.7) | copy-start | bytes 589828
  7.2 18.2 %copy-start.4 = (bf16[16,3,3,2048]{3,0,2,1:T(8,128)(2,1)S(1)}, bf16[16,3,3,2048]{3,0,2,1:T(8,128)(2,1)}, u32[]{:S(2)}) copy-start(bf16[16,3,3,2048]{3,0,2,1:T(8,128)(2,1)} %param.8) | copy-start | bytes 1769476
  7.2 20.1 %copy-start.8 = (s32[15,2048]{1,0:T(8,128)S(1)}, s32[15,2048]{1,0:T(8,128)}, u32[]{:S(2)}) copy-start(s32[15,2048]{1,0:T(8,128)} %param.9) | copy-start | bytes 368644
  7.2 149.4 %all-gather.2.cloned.1.call-start = ((), (), s32[]{:S(2)}) async-start(), calls=%async_computation | async-start | bytes 1769472 | tf_op jit(solution)/shard_map/all_gather | solution.py:53
  12.4 17.2 %collective-permute-start = (bf16[48,512]{0,1:T(8,128)(2,1)S(1)}, bf16[48,512]{0,1:T(8,128)(2,1)S(1)}, u32[]{:S(2)}, u32[]{:S(2)}) collective-permute-start(bf16[48,512]{0,1:T(8,128)(2,1)S(1)} %select_bitcast_fusion.1), channel_id=1, source_target_pairs={{0,8},{8,16},{16,24},{24,32},{32,40},{40,48},{48,56},{56,64},{64,7... | collective-permute-start | bytes 147464 | tf_op jit(solution)/shard_map/ppermute | solution.py:10
  20.6 8.9 %collective-permute-start.1 = (bf16[48,512]{0,1:T(8,128)(2,1)S(1)}, bf16[48,512]{0,1:T(8,128)(2,1)S(1)}, u32[]{:S(2)}, u32[]{:S(2)}) collective-permute-start(bf16[48,512]{0,1:T(8,128)(2,1)S(1)} %select_bitcast_fusion), channel_id=1, source_target_pairs={{8,0},{16,8},{24,16},{32,24},{40,32},{48,40},{56,48},{64,56},{72,6... | collective-permute-start | bytes 147464 | tf_op jit(solution)/shard_map/ppermute | solution.py:10
  154.2 1.0 copy-start.1
  154.2 1.1 copy-start.2
  154.7 1.7 copy-start.5
  154.7 1.7 copy-start.6
  154.7 1.7 copy-start.7
  154.7 1.7 copy-start.9
  154.7 1.7 copy-start.10
  154.7 1.7 copy-start.11
  156.5 131.3 %copy-start.3 = (bf16[16,3,2048]{2,0,1:T(8,128)(2,1)}, bf16[16,3,2048]{2,0,1:T(8,128)(2,1)S(1)}, u32[]{:S(2)}) copy-start(bf16[16,3,2048]{2,0,1:T(8,128)(2,1)S(1)} %add_convert_fusion) | copy-start | bytes 589828
Sparse Core Ops, SparseCore 0:
  10.1 43.8 all-gather.1
where the time goes:
time: 298 us; the launch traced here: 295 us
  blocking collectives  129 us (43%)
  local copies, waits for them, and re-layouts  126 us (42%)
  between operations  14.4 us (5%)
  other arithmetic  12.9 us (4%)
  starting transfers between devices  10.1 us (3%)
    psum x1, blocking collectives, body(): summed_gram = lax.psum(block_terms, 'dom')  129 us
    gather x3, local copies, waits for them, and re-layouts, apply_mass(): gathered = jnp.take(flat_ext, tile_slot.reshape(-1), axis=1)  120 us
    ppermute x2, starting transfers between devices, shifted(): lax.ppermute(value, axis, [(source, source + steps) for source in range(l...  10.1 us
  transfers between devices with their start and end apart: 3, of which 0 were waited for; matrix products, arithmetic and copies ran while one was open for 47% of the time, Pallas kernels for 0%

commit v1 on v0

v1 whole, which is shorter than its diff:
```python
import functools

import jax
import jax.numpy as jnp
from jax import lax
from jax.experimental import pallas as pl
from jax.experimental.pallas import tpu as pltpu
from jax.sharding import PartitionSpec as P

BF16 = jnp.bfloat16
F32 = jnp.float32
MESH = pl.DeviceIdType.MESH

SNAP = 16
NODES = 2048
BLOCK = 256
OWN = NODES // BLOCK
BLOCKS = 12
OTHERS = 15
COLS = 8
EARLY = 2
LAG = 1


def one_hot(low):
    rows = lax.broadcasted_iota(jnp.int16, (BLOCK, low.shape[1]), 0)
    return jnp.where(rows == low.astype(jnp.int16), jnp.array(1, BF16), jnp.array(0, BF16))


def pick(table, slots, first, count):
    low = slots & (BLOCK - 1)
    high = slots >> 8
    stacked = table[first : first + count].reshape(count * 3 * SNAP, BLOCK)
    products = jnp.dot(stacked, one_hot(low), preferred_element_type=F32)
    found = jnp.zeros((3 * SNAP, slots.shape[1]), F32)
    for block in range(count):
        rows = products[block * 3 * SNAP : (block + 1) * 3 * SNAP]
        found = jnp.where(high == first + block, rows, found)
    return found


def kernel(
    snap_ref,
    tiles_ref,
    slot_ref,
    up_ref,
    down_ref,
    mass_ref,
    gram_ref,
    table,
    early,
    all_snap,
    mass_in,
    part_out,
    part_in,
    z_in,
    xc_in,
    halo_send,
    halo_recv,
    snap_send,
    snap_recv,
    mass_send,
    mass_recv,
    part_send,
    part_recv,
    z_send,
    z_recv,
    xc_send,
    xc_recv,
):
    dom = lax.axis_index("dom")
    col = lax.axis_index("col")
    x_pos = dom // 16
    z_pos = (dom // 2) % 8
    core = dom % 2
    xc_pos = x_pos * 2 + core

    def col_peer(step):
        return (dom, lax.rem(col + step, COLS))

    def z_peer(step):
        return (x_pos * 16 + lax.rem(z_pos + step, 8) * 2 + core, col)

    def xc_peer(step):
        other = lax.rem(xc_pos + step, 8)
        return ((other // 2) * 16 + z_pos * 2 + other % 2, col)

    upper = (lax.rem(dom + 1, 64), col)
    lower = (lax.rem(dom + 63, 64), col)

    barrier = pltpu.get_barrier_semaphore()
    for peer in [upper, lower] + [group(step) for step in range(1, 8) for group in (col_peer, z_peer, xc_peer)]:
        pl.semaphore_signal(barrier, inc=1, device_id=peer, device_id_type=MESH)

    for block in range(OWN):
        table[block] = snap_ref[:, :, block * BLOCK : (block + 1) * BLOCK]
    for side, names in ((0, up_ref), (1, down_ref)):
        shared = pick(table, names[...], 0, OWN).astype(BF16)
        for half in range(2):
            for comp in range(3):
                table[BLOCKS + side * 2 + half, comp] = shared[
                    comp * SNAP : (comp + 1) * SNAP, half * BLOCK : (half + 1) * BLOCK
                ]

    pl.semaphore_wait(barrier, 23)

    halo_copies = []
    for side, peer in ((0, upper), (1, lower)):
        copy = pltpu.make_async_remote_copy(
            src_ref=table.at[pl.ds(BLOCKS + 2 * side, 2)],
            dst_ref=table.at[pl.ds(OWN + 2 * side, 2)],
            send_sem=halo_send.at[side],
            recv_sem=halo_recv.at[side],
            device_id=peer,
            device_id_type=MESH,
        )
        copy.start()
        halo_copies.append(copy)
    snap_copies = []
    for step in range(1, COLS):
        target = lax.rem(col + step, COLS)
        copy = pltpu.make_async_remote_copy(
            src_ref=snap_ref.at[:, :, pl.ds(pl.multiple_of(target * BLOCK, BLOCK), BLOCK)],
            dst_ref=all_snap.at[:, pl.ds(pl.multiple_of(col * SNAP, SNAP), SNAP), :],
            send_sem=snap_send.at[step - 1],
            recv_sem=snap_recv.at[step - 1],
            device_id=(dom, target),
            device_id_type=MESH,
        )
        copy.start()
        snap_copies.append(copy)
    all_snap[:, pl.ds(pl.multiple_of(col * SNAP, SNAP), SNAP), :] = table[col]

    def chunk_of(step):
        return lax.rem(col + 1 + step, COLS)

    def columns_of(chunk):
        return pl.ds(pl.multiple_of(chunk * BLOCK, BLOCK), BLOCK)

    def tile_sums(columns, total, own_values, first, count):
        coefs = [[tiles_ref[a, b, :, columns].astype(F32) for b in range(3)] for a in range(3)]
        if own_values is not None:
            for a in range(3):
                for b in range(3):
                    total[a] = total[a] + coefs[a][b][0:1] * own_values[b]
        slots = slot_ref[:, columns]
        for start in range(0, OTHERS, 2):
            ks = range(start, min(start + 2, OTHERS))
            found = pick(table, jnp.concatenate([slots[k : k + 1] for k in ks], axis=1), first, count)
            for place, k in enumerate(ks):
                for a in range(3):
                    for b in range(3):
                        values = found[b * SNAP : (b + 1) * SNAP, place * BLOCK : (place + 1) * BLOCK]
                        total[a] = total[a] + coefs[a][b][k + 1 : k + 2] * values
        return total

    def zeros():
        return [jnp.zeros((SNAP, BLOCK), F32) for _ in range(3)]

    def early_step(step, carry):
        chunk = chunk_of(step)
        total = tile_sums(columns_of(chunk), zeros(), table[chunk].astype(F32), 0, OWN)
        for a in range(3):
            early[step, a] = total[a]
        return carry

    lax.fori_loop(0, EARLY, early_step, 0)

    for copy in halo_copies:
        copy.wait_recv()

    @pl.when(dom == 0)
    def _():
        table[OWN : OWN + 2] = jnp.zeros((2, 3, SNAP, BLOCK), BF16)

    @pl.when(dom == 63)
    def _():
        table[OWN + 2 : OWN + 4] = jnp.zeros((2, 3, SNAP, BLOCK), BF16)

    def mass_copy(step):
        chunk = chunk_of(step)
        return pltpu.make_async_remote_copy(
            src_ref=mass_ref.at[:, :, columns_of(chunk)],
            dst_ref=mass_in.at[step],
            send_sem=mass_send.at[step],
            recv_sem=mass_recv.at[step],
            device_id=(dom, chunk),
            device_id_type=MESH,
        )

    def part_copy(step):
        return pltpu.make_async_remote_copy(
            src_ref=part_out.at[step],
            dst_ref=part_in.at[step],
            send_sem=part_send.at[step],
            recv_sem=part_recv.at[step],
            device_id=(dom, lax.rem(col + 7 - step, COLS)),
            device_id_type=MESH,
        )

    def products(rows):
        total = None
        for a in range(3):
            term = lax.dot_general(
                rows[a], all_snap[a], (((1,), (1,)), ((), ())), preferred_element_type=F32
            )
            total = term if total is None else total + term
        return total

    def finish(step, total):
        columns = columns_of(chunk_of(step))
        for a in range(3):
            mass_ref[a, :, columns] = total[a].astype(BF16)

        @pl.when(step < COLS - 1)
        def _():
            mass_copy(step).start()

    def answer(step):
        mass_copy(step).wait_recv()
        part_out[step] = products(mass_in[step])
        part_copy(step).start()

    def late_step(step, carry):
        columns = columns_of(chunk_of(step))
        total = tile_sums(columns, [early[step, a] for a in range(3)], None, OWN, BLOCKS - OWN)
        finish(step, total)
        return carry

    lax.fori_loop(0, EARLY, late_step, 0)

    for copy in snap_copies:
        copy.wait_recv()

    def full_step(step, carry):
        chunk = chunk_of(step)
        total = tile_sums(columns_of(chunk), zeros(), table[chunk].astype(F32), 0, BLOCKS)
        finish(step, total)
        answer(step - LAG)
        return carry

    for step in range(EARLY - LAG):
        answer(jnp.int32(step))
    lax.fori_loop(EARLY, COLS, full_step, 0)
    for step in range(COLS - LAG, COLS - 1):
        answer(jnp.int32(step))

    own_part = products(mass_ref[:, :, columns_of(col)])
    for step in range(COLS - 1):
        part_copy(step).wait_recv()
        own_part = own_part + part_in[step]

    def exchange(value, place, slots, peer_of, sends, recvs):
        slots[place] = value
        copies = []
        for step in range(1, 8):
            copy = pltpu.make_async_remote_copy(
                src_ref=slots.at[place],
                dst_ref=slots.at[place],
                send_sem=sends.at[step - 1],
                recv_sem=recvs.at[step - 1],
                device_id=peer_of(step),
                device_id_type=MESH,
            )
            copy.start()
            copies.append(copy)
        for copy in copies:
            copy.wait_recv()
        total = slots[0]
        for other in range(1, 8):
            total = total + slots[other]
        return total, copies

    z_sum, z_copies = exchange(own_part, z_pos, z_in, z_peer, z_send, z_recv)
    xc_sum, xc_copies = exchange(z_sum, xc_pos, xc_in, xc_peer, xc_send, xc_recv)
    gram_ref[...] = xc_sum / (3.0 * NODES * 64)

    for copy in halo_copies + snap_copies + z_copies + xc_copies:
        copy.wait_send()
    for step in range(COLS - 1):
        mass_copy(step).wait_send()
        part_copy(step).wait_send()


def body(snapshots, mass_tiles, tile_slot, send_up, send_down):
    vmem = pl.BlockSpec(memory_space=pltpu.VMEM)
    dma = pltpu.SemaphoreType.DMA
    mass, gram = pl.pallas_call(
        kernel,
        out_shape=(
            jax.ShapeDtypeStruct((3, SNAP, NODES), BF16),
            jax.ShapeDtypeStruct((SNAP, COLS * SNAP), F32),
        ),
        in_specs=[vmem] * 5,
        out_specs=(vmem, vmem),
        scratch_shapes=[
            pltpu.VMEM((BLOCKS + 4, 3, SNAP, BLOCK), BF16),
            pltpu.VMEM((EARLY, 3, SNAP, BLOCK), F32),
            pltpu.VMEM((3, COLS * SNAP, BLOCK), BF16),
            pltpu.VMEM((COLS - 1, 3, SNAP, BLOCK), BF16),
            pltpu.VMEM((COLS - 1, SNAP, COLS * SNAP), F32),
            pltpu.VMEM((COLS - 1, SNAP, COLS * SNAP), F32),
            pltpu.VMEM((8, SNAP, COLS * SNAP), F32),
            pltpu.VMEM((8, SNAP, COLS * SNAP), F32),
            dma((2,)),
            dma((2,)),
        ]
        + [dma((7,))] * 10,
        compiler_params=pltpu.CompilerParams(
            collective_id=0, has_side_effects=True, vmem_limit_bytes=32 * 2**20
        ),
        cost_estimate=pl.CostEstimate(flops=9_100_000_000, bytes_accessed=1_200_000, transcendentals=0),
    )(
        jnp.transpose(snapshots, (1, 0, 2)),
        jnp.transpose(mass_tiles, (1, 2, 0, 3)),
        tile_slot,
        send_up.reshape(1, -1),
        send_down.reshape(1, -1),
    )
    return jnp.transpose(mass, (1, 0, 2)), jnp.transpose(gram, (1, 0))


def solution(mesh):
    placed = (P("col", None, "dom"), P(None, None, None, "dom"), P(None, "dom"), P("dom"), P("dom"))
    return jax.shard_map(
        body,
        mesh=mesh,
        in_specs=placed,
        out_specs=(P("col", None, "dom"), P(None, "col")),
        check_vma=False,
    )
```

time: 298 us -> 58.3 us (0.20); the launches traced: 295 us -> 58.1 us
  blocking collectives: 129 us -> 0 us
  local copies, waits for them, and re-layouts: 126 us -> 4.85 us
  Pallas kernels: 0 us -> 52.6 us
  between operations: 14.4 us -> 0.66 us
  other arithmetic: 12.9 us -> 0 us
  starting transfers between devices: 10.1 us -> 0 us
    psum x1 -> x0, blocking collectives: 129 us -> none  [body(): summed_gram = lax.psum(block_terms, 'dom')]
    gather x5 -> x0, local copies, waits for them, and re-layouts: 122 us -> none  [the longest x3 120 us: apply_mass(): gathered = jnp.take(flat_ext, tile_slot.reshape(-1), axis=1)]
    pallas_call x0 -> x1, Pallas kernels: none -> 52.6 us  [body(): pl.pallas_call(kernel, out_shape=(jax.ShapeDtypeStruct((3, SNAP, NODES),...]
    ppermute x2 -> x0, starting transfers between devices: 10.1 us -> none  [shifted(): lax.ppermute(value, axis, [(source, source + steps) for source in range(l...]
    select_n x6 -> x0, other arithmetic: 6.1 us -> none  [the longest x2 4.45 us: apply_mass(): gathered = jnp.take(flat_ext, tile_slot.reshape(-1), axis=1)]
  transfers between devices with their start and end apart: 3 -> 0, of which waited for: 0 -> 0; matrix products, arithmetic and copies ran while one was open for 47% -> 0% of each run, Pallas kernels for 0% -> 0%
where the time goes in v1:
time: 58.3 us; the launch traced here: 58.1 us
  Pallas kernels  52.6 us (90%)
  local copies, waits for them, and re-layouts  4.85 us (8%)
  between operations  0.66 us (1%)
    pallas_call x1, Pallas kernels, body(): pl.pallas_call(kernel, out_shape=(jax.ShapeDtypeStruct((3, SNAP, NODES),...  52.6 us
    unnamed x12, local copies, waits for them, and re-layouts  4.85 us

profile of v1, /device:TPU:1, one launch (start us, length us, event | category | flops | bytes accessed | tf_op | source)
XLA Modules:
  0.0 58.1 jit_solution(10205670267701028320)
XLA Ops:
  0.6 0.0 copy-start.4
  0.6 0.0 copy-start.3
  0.7 0.7 %copy-done.4 = s32[512]{0:T(512)S(1)} copy-done((s32[512]{0:T(512)S(1)}, s32[512]{0:T(512)}, u32[]{:S(2)}) %copy-start.4) | copy-done | bytes 2072
  1.3 0.0 copy-done.3
  1.3 0.0 copy-start
  1.3 1.1 %copy-done = bf16[16,3,3,2048]{3,0,2,1:T(8,128)(2,1)S(1)} copy-done((bf16[16,3,3,2048]{3,0,2,1:T(8,128)(2,1)S(1)}, bf16[16,3,3,2048]{3,0,2,1:T(8,128)(2,1)}, u32[]{:S(2)}) %copy-start) | copy-done | bytes 589848
  2.4 0.0 copy-start.1
  2.4 0.9 %copy-done.1 = bf16[16,3,2048]{2,0,1:T(8,128)(2,1)S(1)} copy-done((bf16[16,3,2048]{2,0,1:T(8,128)(2,1)S(1)}, bf16[16,3,2048]{2,0,1:T(8,128)(2,1)}, u32[]{:S(2)}) %copy-start.1) | copy-done | bytes 196632
  3.3 0.0 copy-start.2
  3.3 0.9 %copy-done.2 = s32[15,2048]{1,0:T(8,128)S(1)} copy-done((s32[15,2048]{1,0:T(8,128)S(1)}, s32[15,2048]{1,0:T(8,128)}, u32[]{:S(2)}) %copy-start.2) | copy-done | bytes 122904
  4.2 52.6 %shard_map.68 = (bf16[3,16,2048]{2,1,0:T(8,128)(2,1)S(1)}, f32[16,128]{1,0:T(8,128)S(1)}) custom-call(bf16[3,16,2048]{2,1,0:T(8,128)(2,1)S(1)} %bitcast.9, bf16[3,3,16,2048]{3,2,1,0:T(8,128)(2,1)S(1)} %bitcast.8, s32[15,2048]{1,0:T(8,128)S(1)} %copy-done.2, s32[1,512]{1,0:T(1,128)S(1)} %bitcast.10, s32[1,512]{1,0:T(1,128)S(1)} %bitcast.11), custom_call_target="tpu_custom_call" | custom-call | flops 9100000256 | bytes 1200000 | tf_op jit(solution)/shard_map/pallas_call | solution.py:288
  56.8 0.7 %copy.9 = bf16[16,3,2048]{2,0,1:T(8,128)(2,1)} copy(bf16[16,3,2048]{2,0,1:T(8,128)(2,1)S(1)} %bitcast.6) | data formatting | bytes 393216
  57.5 0.6 %copy.10 = f32[128,16]{0,1:T(8,128)} copy(f32[128,16]{0,1:T(8,128)S(1)} %bitcast.7) | data formatting | bytes 16384
Async XLA Ops:
  0.6 0.7 %copy-start.4 = (s32[512]{0:T(512)S(1)}, s32[512]{0:T(512)}, u32[]{:S(2)}) copy-start(s32[512]{0:T(512)} %param.9) | copy-start | bytes 6148
  0.6 0.7 %copy-start.3 = (s32[512]{0:T(512)S(1)}, s32[512]{0:T(512)}, u32[]{:S(2)}) copy-start(s32[512]{0:T(512)} %param.8) | copy-start | bytes 6148
  1.3 1.1 %copy-start = (bf16[16,3,3,2048]{3,0,2,1:T(8,128)(2,1)S(1)}, bf16[16,3,3,2048]{3,0,2,1:T(8,128)(2,1)}, u32[]{:S(2)}) copy-start(bf16[16,3,3,2048]{3,0,2,1:T(8,128)(2,1)} %param.6) | copy-start | bytes 1769476
  2.4 0.9 %copy-start.1 = (bf16[16,3,2048]{2,0,1:T(8,128)(2,1)S(1)}, bf16[16,3,2048]{2,0,1:T(8,128)(2,1)}, u32[]{:S(2)}) copy-start(bf16[16,3,2048]{2,0,1:T(8,128)(2,1)} %param.5) | copy-start | bytes 589828
  3.3 0.9 %copy-start.2 = (s32[15,2048]{1,0:T(8,128)S(1)}, s32[15,2048]{1,0:T(8,128)}, u32[]{:S(2)}) copy-start(s32[15,2048]{1,0:T(8,128)} %slot_ref.1) | copy-start | bytes 368644

commit v2 on v1

--- a/solution.py
+++ b/solution.py
@@ -18,8 +18,9 @@
 BLOCKS = 12
 OTHERS = 15
 COLS = 8
-EARLY = 2
-LAG = 1
+BEFORE = 2
+EARLY = 4
+FIRST_ANSWERS = 5
 
 
 def one_hot(low):
@@ -40,14 +41,18 @@
 
 
 def kernel(
-    snap_ref,
+    snap_hbm,
+    tiles_hbm,
+    slot_hbm,
+    up_hbm,
+    down_hbm,
+    mass_ref,
+    gram_ref,
+    table,
     tiles_ref,
     slot_ref,
     up_ref,
     down_ref,
-    mass_ref,
-    gram_ref,
-    table,
     early,
     all_snap,
     mass_in,
@@ -55,6 +60,8 @@
     part_in,
     z_in,
     xc_in,
+    load_snap,
+    load_rest,
     halo_send,
     halo_recv,
     snap_send,
@@ -88,12 +95,29 @@
     upper = (lax.rem(dom + 1, 64), col)
     lower = (lax.rem(dom + 63, 64), col)
 
+    snap_loads = [
+        pltpu.make_async_copy(
+            snap_hbm.at[:, :, pl.ds(block * BLOCK, BLOCK)], table.at[block], load_snap.at[block]
+        )
+        for block in range(OWN)
+    ]
+    name_loads = [
+        pltpu.make_async_copy(up_hbm, up_ref, load_rest.at[0]),
+        pltpu.make_async_copy(down_hbm, down_ref, load_rest.at[1]),
+    ]
+    tile_loads = [
+        pltpu.make_async_copy(slot_hbm, slot_ref, load_rest.at[2]),
+        pltpu.make_async_copy(tiles_hbm, tiles_ref, load_rest.at[3]),
+    ]
+    for load in name_loads + snap_loads + tile_loads:
+        load.start()
+
     barrier = pltpu.get_barrier_semaphore()
     for peer in [upper, lower] + [group(step) for step in range(1, 8) for group in (col_peer, z_peer, xc_peer)]:
         pl.semaphore_signal(barrier, inc=1, device_id=peer, device_id_type=MESH)
 
-    for block in range(OWN):
-        table[block] = snap_ref[:, :, block * BLOCK : (block + 1) * BLOCK]
+    for load in name_loads + snap_loads:
+        load.wait()
     for side, names in ((0, up_ref), (1, down_ref)):
         shared = pick(table, names[...], 0, OWN).astype(BF16)
         for half in range(2):
@@ -102,37 +126,11 @@
                     comp * SNAP : (comp + 1) * SNAP, half * BLOCK : (half + 1) * BLOCK
                 ]
 
-    pl.semaphore_wait(barrier, 23)
-
-    halo_copies = []
-    for side, peer in ((0, upper), (1, lower)):
-        copy = pltpu.make_async_remote_copy(
-            src_ref=table.at[pl.ds(BLOCKS + 2 * side, 2)],
-            dst_ref=table.at[pl.ds(OWN + 2 * side, 2)],
-            send_sem=halo_send.at[side],
-            recv_sem=halo_recv.at[side],
-            device_id=peer,
-            device_id_type=MESH,
-        )
-        copy.start()
-        halo_copies.append(copy)
-    snap_copies = []
-    for step in range(1, COLS):
-        target = lax.rem(col + step, COLS)
-        copy = pltpu.make_async_remote_copy(
-            src_ref=snap_ref.at[:, :, pl.ds(pl.multiple_of(target * BLOCK, BLOCK), BLOCK)],
-            dst_ref=all_snap.at[:, pl.ds(pl.multiple_of(col * SNAP, SNAP), SNAP), :],
-            send_sem=snap_send.at[step - 1],
-            recv_sem=snap_recv.at[step - 1],
-            device_id=(dom, target),
-            device_id_type=MESH,
-        )
-        copy.start()
-        snap_copies.append(copy)
-    all_snap[:, pl.ds(pl.multiple_of(col * SNAP, SNAP), SNAP), :] = table[col]
+    def offset_of(step):
+        return 4 + (1 - 2 * lax.rem(step, 2)) * lax.div(step + 1, 2)
 
     def chunk_of(step):
-        return lax.rem(col + 1 + step, COLS)
+        return lax.rem(col + offset_of(step), COLS)
 
     def columns_of(chunk):
         return pl.ds(pl.multiple_of(chunk * BLOCK, BLOCK), BLOCK)
@@ -164,7 +162,40 @@
             early[step, a] = total[a]
         return carry
 
-    lax.fori_loop(0, EARLY, early_step, 0)
+    for load in tile_loads:
+        load.wait()
+    lax.fori_loop(0, BEFORE, early_step, 0)
+
+    pl.semaphore_wait(barrier, 23)
+
+    halo_copies = []
+    for side, peer in ((0, upper), (1, lower)):
+        copy = pltpu.make_async_remote_copy(
+            src_ref=table.at[pl.ds(BLOCKS + 2 * side, 2)],
+            dst_ref=table.at[pl.ds(OWN + 2 * side, 2)],
+            send_sem=halo_send.at[side],
+            recv_sem=halo_recv.at[side],
+            device_id=peer,
+            device_id_type=MESH,
+        )
+        copy.start()
+        halo_copies.append(copy)
+    snap_copies = []
+    for step in range(1, COLS):
+        target = lax.rem(col + step, COLS)
+        copy = pltpu.make_async_remote_copy(
+            src_ref=table.at[target],
+            dst_ref=all_snap.at[:, pl.ds(pl.multiple_of(col * SNAP, SNAP), SNAP), :],
+            send_sem=snap_send.at[step - 1],
+            recv_sem=snap_recv.at[step - 1],
+            device_id=(dom, target),
+            device_id_type=MESH,
+        )
+        copy.start()
+        snap_copies.append(copy)
+    all_snap[:, pl.ds(pl.multiple_of(col * SNAP, SNAP), SNAP), :] = table[col]
+
+    lax.fori_loop(BEFORE, EARLY, early_step, 0)
 
     for copy in halo_copies:
         copy.wait_recv()
@@ -194,16 +225,15 @@
             dst_ref=part_in.at[step],
             send_sem=part_send.at[step],
             recv_sem=part_recv.at[step],
-            device_id=(dom, lax.rem(col + 7 - step, COLS)),
+            device_id=(dom, lax.rem(col + COLS - offset_of(step), COLS)),
             device_id_type=MESH,
         )
 
-    def products(rows):
+    def products(first, last):
         total = None
         for a in range(3):
-            term = lax.dot_general(
-                rows[a], all_snap[a], (((1,), (1,)), ((), ())), preferred_element_type=F32
-            )
+            rows = mass_in[first:last, a].reshape((last - first) * SNAP, BLOCK)
+            term = lax.dot_general(rows, all_snap[a], (((1,), (1,)), ((), ())), preferred_element_type=F32)
             total = term if total is None else total + term
         return total
 
@@ -216,10 +246,14 @@
         def _():
             mass_copy(step).start()
 
-    def answer(step):
-        mass_copy(step).wait_recv()
-        part_out[step] = products(mass_in[step])
-        part_copy(step).start()
+    def answer(first, last, also_own):
+        for step in range(first, last):
+            mass_copy(step).wait_recv()
+        total = products(first, last + 1 if also_own else last)
+        for step in range(first, last):
+            part_out[step] = total[(step - first) * SNAP : (step - first + 1) * SNAP]
+            part_copy(step).start()
+        return total[(last - first) * SNAP :]
 
     def late_step(step, carry):
         columns = columns_of(chunk_of(step))
@@ -229,23 +263,23 @@
 
     lax.fori_loop(0, EARLY, late_step, 0)
 
-    for copy in snap_copies:
-        copy.wait_recv()
-
     def full_step(step, carry):
         chunk = chunk_of(step)
         total = tile_sums(columns_of(chunk), zeros(), table[chunk].astype(F32), 0, BLOCKS)
         finish(step, total)
-        answer(step - LAG)
+
+        @pl.when(step == COLS - 2)
+        def _():
+            for copy in snap_copies:
+                copy.wait_recv()
+            answer(0, FIRST_ANSWERS, False)
+
         return carry
 
-    for step in range(EARLY - LAG):
-        answer(jnp.int32(step))
     lax.fori_loop(EARLY, COLS, full_step, 0)
-    for step in range(COLS - LAG, COLS - 1):
-        answer(jnp.int32(step))
-
-    own_part = products(mass_ref[:, :, columns_of(col)])
+
+    mass_in[COLS - 1] = mass_ref[:, :, columns_of(col)]
+    own_part = answer(FIRST_ANSWERS, COLS - 1, True)
     for step in range(COLS - 1):
         part_copy(step).wait_recv()
         own_part = own_part + part_in[step]
@@ -291,17 +325,23 @@
             jax.ShapeDtypeStruct((3, SNAP, NODES), BF16),
             jax.ShapeDtypeStruct((SNAP, COLS * SNAP), F32),
         ),
-        in_specs=[vmem] * 5,
+        in_specs=[pl.BlockSpec(memory_space=pltpu.HBM)] * 5,
         out_specs=(vmem, vmem),
         scratch_shapes=[
             pltpu.VMEM((BLOCKS + 4, 3, SNAP, BLOCK), BF16),
+            pltpu.VMEM((3, 3, OTHERS + 1, NODES), BF16),
+            pltpu.VMEM((OTHERS, NODES), jnp.int32),
+            pltpu.VMEM((1, 2 * BLOCK), jnp.int32),
+            pltpu.VMEM((1, 2 * BLOCK), jnp.int32),
             pltpu.VMEM((EARLY, 3, SNAP, BLOCK), F32),
             pltpu.VMEM((3, COLS * SNAP, BLOCK), BF16),
-            pltpu.VMEM((COLS - 1, 3, SNAP, BLOCK), BF16),
+            pltpu.VMEM((COLS, 3, SNAP, BLOCK), BF16),
             pltpu.VMEM((COLS - 1, SNAP, COLS * SNAP), F32),
             pltpu.VMEM((COLS - 1, SNAP, COLS * SNAP), F32),
             pltpu.VMEM((8, SNAP, COLS * SNAP), F32),
             pltpu.VMEM((8, SNAP, COLS * SNAP), F32),
+            dma((OWN,)),
+            dma((4,)),
             dma((2,)),
             dma((2,)),
         ]
@@ -311,11 +351,16 @@
         ),
         cost_estimate=pl.CostEstimate(flops=9_100_000_000, bytes_accessed=1_200_000, transcendentals=0),
     )(
-        jnp.transpose(snapshots, (1, 0, 2)),
-        jnp.transpose(mass_tiles, (1, 2, 0, 3)),
-        tile_slot,
-        send_up.reshape(1, -1),
-        send_down.reshape(1, -1),
+        *(
+            pltpu.with_memory_space_constraint(operand, pltpu.HBM)
+            for operand in (
+                jnp.transpose(snapshots, (1, 0, 2)),
+                jnp.transpose(mass_tiles, (1, 2, 0, 3)),
+                tile_slot,
+                send_up.reshape(1, -1),
+                send_down.reshape(1, -1),
+            )
+        )
     )
     return jnp.transpose(mass, (1, 0, 2)), jnp.transpose(gram, (1, 0))
 

time: 58.3 us -> 43 us (0.74)
  Pallas kernels: 52.6 us -> 41 us
  local copies, waits for them, and re-layouts: 4.85 us -> 1.28 us
    pallas_call x1, Pallas kernels: 52.6 us -> 41 us  [body(): pl.pallas_call(kernel, out_shape=(jax.ShapeDtypeStruct((3, SNAP, NODES),...]
    unnamed x12 -> x2, local copies, waits for them, and re-layouts: 4.85 us -> 1.28 us
where the time goes in v2:
time: 43 us; the launch traced here: 42.9 us
  Pallas kernels  41 us (95%)
  local copies, waits for them, and re-layouts  1.28 us (3%)
  between operations  0.64 us (1%)
    pallas_call x1, Pallas kernels, body(): pl.pallas_call(kernel, out_shape=(jax.ShapeDtypeStruct((3, SNAP, NODES),...  41 us
    unnamed x2, local copies, waits for them, and re-layouts  1.28 us

profile of v2, /device:TPU:1, one launch (start us, length us, event | category | flops | bytes accessed | tf_op | source)
XLA Modules:
  0.0 42.9 jit_solution(1469675496437400751)
XLA Ops:
  0.6 41.0 %shard_map.68 = (bf16[3,16,2048]{2,1,0:T(8,128)(2,1)S(1)}, f32[16,128]{1,0:T(8,128)S(1)}) custom-call(bf16[3,16,2048]{2,1,0:T(8,128)(2,1)} %bitcast.9, bf16[3,3,16,2048]{3,2,1,0:T(8,128)(2,1)} %bitcast.8, s32[15,2048]{1,0:T(8,128)} %slot_hbm.1, s32[1,512]{1,0:T(1,128)} %bitcast.10, s32[1,512]{1,0:T(1,128)} %bitcast.11), custom_call_target="tpu_custom_call" | custom-call | flops 9100000256 | bytes 1200000 | tf_op jit(solution)/shard_map/pallas_call | solution.py:322
  41.6 0.7 %copy.9 = bf16[16,3,2048]{2,0,1:T(8,128)(2,1)} copy(bf16[16,3,2048]{2,0,1:T(8,128)(2,1)S(1)} %bitcast.6) | data formatting | bytes 393216
  42.3 0.6 %copy.10 = f32[128,16]{0,1:T(8,128)} copy(f32[128,16]{0,1:T(8,128)S(1)} %bitcast.7) | data formatting | bytes 16384

commit v3 on v2

--- a/solution.py
+++ b/solution.py
@@ -20,6 +20,7 @@
 COLS = 8
 BEFORE = 2
 EARLY = 4
+FAR_FIRST = (4, 3, 5, 2, 6, 1, 7)
 FIRST_ANSWERS = 5
 
 
@@ -113,7 +114,7 @@
         load.start()
 
     barrier = pltpu.get_barrier_semaphore()
-    for peer in [upper, lower] + [group(step) for step in range(1, 8) for group in (col_peer, z_peer, xc_peer)]:
+    for peer in [group(step) for group in (col_peer, z_peer, xc_peer) for step in FAR_FIRST] + [upper, lower]:
         pl.semaphore_signal(barrier, inc=1, device_id=peer, device_id_type=MESH)
 
     for load in name_loads + snap_loads:
@@ -164,26 +165,19 @@
 
     for load in tile_loads:
         load.wait()
-    lax.fori_loop(0, BEFORE, early_step, 0)
-
-    pl.semaphore_wait(barrier, 23)
-
-    halo_copies = []
-    for side, peer in ((0, upper), (1, lower)):
-        copy = pltpu.make_async_remote_copy(
+    def halo_copy(side):
+        return pltpu.make_async_remote_copy(
             src_ref=table.at[pl.ds(BLOCKS + 2 * side, 2)],
             dst_ref=table.at[pl.ds(OWN + 2 * side, 2)],
             send_sem=halo_send.at[side],
             recv_sem=halo_recv.at[side],
-            device_id=peer,
+            device_id=(upper, lower)[side],
             device_id_type=MESH,
         )
-        copy.start()
-        halo_copies.append(copy)
-    snap_copies = []
-    for step in range(1, COLS):
+
+    def snap_copy(step):
         target = lax.rem(col + step, COLS)
-        copy = pltpu.make_async_remote_copy(
+        return pltpu.make_async_remote_copy(
             src_ref=table.at[target],
             dst_ref=all_snap.at[:, pl.ds(pl.multiple_of(col * SNAP, SNAP), SNAP), :],
             send_sem=snap_send.at[step - 1],
@@ -191,14 +185,25 @@
             device_id=(dom, target),
             device_id_type=MESH,
         )
-        copy.start()
-        snap_copies.append(copy)
-    all_snap[:, pl.ds(pl.multiple_of(col * SNAP, SNAP), SNAP), :] = table[col]
-
-    lax.fori_loop(BEFORE, EARLY, early_step, 0)
-
-    for copy in halo_copies:
-        copy.wait_recv()
+
+    def early_and_send(step, carry):
+        early_step(step, carry)
+
+        @pl.when(step == BEFORE - 1)
+        def _():
+            pl.semaphore_wait(barrier, 23)
+            for side in range(2):
+                halo_copy(side).start()
+            for peer_step in FAR_FIRST:
+                snap_copy(peer_step).start()
+            all_snap[:, pl.ds(pl.multiple_of(col * SNAP, SNAP), SNAP), :] = table[col]
+
+        return carry
+
+    lax.fori_loop(0, EARLY, early_and_send, 0)
+
+    for side in range(2):
+        halo_copy(side).wait_recv()
 
     @pl.when(dom == 0)
     def _():
@@ -270,8 +275,8 @@
 
         @pl.when(step == COLS - 2)
         def _():
-            for copy in snap_copies:
-                copy.wait_recv()
+            for peer_step in FAR_FIRST:
+                snap_copy(peer_step).wait_recv()
             answer(0, FIRST_ANSWERS, False)
 
         return carry
@@ -287,7 +292,7 @@
     def exchange(value, place, slots, peer_of, sends, recvs):
         slots[place] = value
         copies = []
-        for step in range(1, 8):
+        for step in FAR_FIRST:
             copy = pltpu.make_async_remote_copy(
                 src_ref=slots.at[place],
                 dst_ref=slots.at[place],
@@ -309,8 +314,12 @@
     xc_sum, xc_copies = exchange(z_sum, xc_pos, xc_in, xc_peer, xc_send, xc_recv)
     gram_ref[...] = xc_sum / (3.0 * NODES * 64)
 
-    for copy in halo_copies + snap_copies + z_copies + xc_copies:
+    for copy in z_copies + xc_copies:
         copy.wait_send()
+    for side in range(2):
+        halo_copy(side).wait_send()
+    for peer_step in FAR_FIRST:
+        snap_copy(peer_step).wait_send()
     for step in range(COLS - 1):
         mass_copy(step).wait_send()
         part_copy(step).wait_send()

time: 43 us -> 42.9 us (level)
  no operation moved by 1% of the time
where the time goes in v3:
time: 42.9 us; the launch traced here: 42.7 us
  Pallas kernels  40.8 us (95%)
  local copies, waits for them, and re-layouts  1.28 us (3%)
  between operations  0.64 us (1%)
    pallas_call x1, Pallas kernels, body(): pl.pallas_call(kernel, out_shape=(jax.ShapeDtypeStruct((3, SNAP, NODES),...  40.8 us
    unnamed x2, local copies, waits for them, and re-layouts  1.28 us

profile of v3, /device:TPU:1, one launch (start us, length us, event | category | flops | bytes accessed | tf_op | source)
XLA Modules:
  0.0 42.7 jit_solution(13100235928947011075)
XLA Ops:
  0.6 40.8 %shard_map.68 = (bf16[3,16,2048]{2,1,0:T(8,128)(2,1)S(1)}, f32[16,128]{1,0:T(8,128)S(1)}) custom-call(bf16[3,16,2048]{2,1,0:T(8,128)(2,1)} %bitcast.9, bf16[3,3,16,2048]{3,2,1,0:T(8,128)(2,1)} %bitcast.8, s32[15,2048]{1,0:T(8,128)} %slot_hbm.1, s32[1,512]{1,0:T(1,128)} %bitcast.10, s32[1,512]{1,0:T(1,128)} %bitcast.11), custom_call_target="tpu_custom_call" | custom-call | flops 9100000256 | bytes 1200000 | tf_op jit(solution)/shard_map/pallas_call | solution.py:331
  41.5 0.7 %copy.9 = bf16[16,3,2048]{2,0,1:T(8,128)(2,1)} copy(bf16[16,3,2048]{2,0,1:T(8,128)(2,1)S(1)} %bitcast.6) | data formatting | bytes 393216
  42.1 0.6 %copy.10 = f32[128,16]{0,1:T(8,128)} copy(f32[128,16]{0,1:T(8,128)S(1)} %bitcast.7) | data formatting | bytes 16384

commit v4 on v3

--- a/solution.py
+++ b/solution.py
@@ -21,6 +21,7 @@
 BEFORE = 2
 EARLY = 4
 FAR_FIRST = (4, 3, 5, 2, 6, 1, 7)
+X_STEPS = (2, 1, 3)
 FIRST_ANSWERS = 5
 
 
@@ -60,7 +61,7 @@
     part_out,
     part_in,
     z_in,
-    xc_in,
+    x_in,
     load_snap,
     load_rest,
     halo_send,
@@ -73,15 +74,14 @@
     part_recv,
     z_send,
     z_recv,
-    xc_send,
-    xc_recv,
+    x_send,
+    x_recv,
 ):
     dom = lax.axis_index("dom")
     col = lax.axis_index("col")
     x_pos = dom // 16
     z_pos = (dom // 2) % 8
     core = dom % 2
-    xc_pos = x_pos * 2 + core
 
     def col_peer(step):
         return (dom, lax.rem(col + step, COLS))
@@ -89,9 +89,10 @@
     def z_peer(step):
         return (x_pos * 16 + lax.rem(z_pos + step, 8) * 2 + core, col)
 
-    def xc_peer(step):
-        other = lax.rem(xc_pos + step, 8)
-        return ((other // 2) * 16 + z_pos * 2 + other % 2, col)
+    def x_peer(step):
+        return (lax.rem(x_pos + step, 4) * 16 + z_pos * 2 + core, col)
+
+    sibling = dom + 1 - 2 * core
 
     upper = (lax.rem(dom + 1, 64), col)
     lower = (lax.rem(dom + 63, 64), col)
@@ -114,7 +115,9 @@
         load.start()
 
     barrier = pltpu.get_barrier_semaphore()
-    for peer in [group(step) for group in (col_peer, z_peer, xc_peer) for step in FAR_FIRST] + [upper, lower]:
+    peers = [group(step) for group in (col_peer, z_peer) for step in FAR_FIRST]
+    peers += [x_peer(step) for step in X_STEPS] + [(sibling, other) for other in range(COLS)] + [upper, lower]
+    for peer in peers:
         pl.semaphore_signal(barrier, inc=1, device_id=peer, device_id_type=MESH)
 
     for load in name_loads + snap_loads:
@@ -191,7 +194,7 @@
 
         @pl.when(step == BEFORE - 1)
         def _():
-            pl.semaphore_wait(barrier, 23)
+            pl.semaphore_wait(barrier, len(peers))
             for side in range(2):
                 halo_copy(side).start()
             for peer_step in FAR_FIRST:
@@ -224,13 +227,13 @@
             device_id_type=MESH,
         )
 
-    def part_copy(step):
+    def part_copy(step, side, source):
         return pltpu.make_async_remote_copy(
             src_ref=part_out.at[step],
-            dst_ref=part_in.at[step],
-            send_sem=part_send.at[step],
-            recv_sem=part_recv.at[step],
-            device_id=(dom, lax.rem(col + COLS - offset_of(step), COLS)),
+            dst_ref=part_in.at[source, step],
+            send_sem=part_send.at[side, step],
+            recv_sem=part_recv.at[source, step],
+            device_id=((dom, sibling)[side], lax.rem(col + COLS - offset_of(step), COLS)),
             device_id_type=MESH,
         )
 
@@ -257,7 +260,8 @@
         total = products(first, last + 1 if also_own else last)
         for step in range(first, last):
             part_out[step] = total[(step - first) * SNAP : (step - first + 1) * SNAP]
-            part_copy(step).start()
+            for side in range(2):
+                part_copy(step, side, core).start()
         return total[(last - first) * SNAP :]
 
     def late_step(step, carry):
@@ -285,14 +289,21 @@
 
     mass_in[COLS - 1] = mass_ref[:, :, columns_of(col)]
     own_part = answer(FIRST_ANSWERS, COLS - 1, True)
+    part_out[COLS - 1] = own_part
+    part_copy(COLS - 1, 1, core).start()
+    part_in[core, COLS - 1] = own_part
     for step in range(COLS - 1):
-        part_copy(step).wait_recv()
-        own_part = own_part + part_in[step]
-
-    def exchange(value, place, slots, peer_of, sends, recvs):
+        part_copy(step, 0, core).wait_recv()
+        part_copy(step, 1, 1 - core).wait_recv()
+    part_copy(COLS - 1, 1, 1 - core).wait_recv()
+    chip_part = part_in[0, 0]
+    for place in range(1, 2 * COLS):
+        chip_part = chip_part + part_in[place // COLS, place % COLS]
+
+    def exchange(value, place, slots, steps, peer_of, sends, recvs):
         slots[place] = value
         copies = []
-        for step in FAR_FIRST:
+        for step in steps:
             copy = pltpu.make_async_remote_copy(
                 src_ref=slots.at[place],
                 dst_ref=slots.at[place],
@@ -306,15 +317,15 @@
         for copy in copies:
             copy.wait_recv()
         total = slots[0]
-        for other in range(1, 8):
+        for other in range(1, len(steps) + 1):
             total = total + slots[other]
         return total, copies
 
-    z_sum, z_copies = exchange(own_part, z_pos, z_in, z_peer, z_send, z_recv)
-    xc_sum, xc_copies = exchange(z_sum, xc_pos, xc_in, xc_peer, xc_send, xc_recv)
-    gram_ref[...] = xc_sum / (3.0 * NODES * 64)
-
-    for copy in z_copies + xc_copies:
+    z_sum, z_copies = exchange(chip_part, z_pos, z_in, FAR_FIRST, z_peer, z_send, z_recv)
+    x_sum, x_copies = exchange(z_sum, x_pos, x_in, X_STEPS, x_peer, x_send, x_recv)
+    gram_ref[...] = x_sum / (3.0 * NODES * 64)
+
+    for copy in z_copies + x_copies:
         copy.wait_send()
     for side in range(2):
         halo_copy(side).wait_send()
@@ -322,7 +333,9 @@
         snap_copy(peer_step).wait_send()
     for step in range(COLS - 1):
         mass_copy(step).wait_send()
-        part_copy(step).wait_send()
+        part_copy(step, 0, core).wait_send()
+        part_copy(step, 1, core).wait_send()
+    part_copy(COLS - 1, 1, core).wait_send()
 
 
 def body(snapshots, mass_tiles, tile_slot, send_up, send_down):
@@ -345,16 +358,18 @@
             pltpu.VMEM((EARLY, 3, SNAP, BLOCK), F32),
             pltpu.VMEM((3, COLS * SNAP, BLOCK), BF16),
             pltpu.VMEM((COLS, 3, SNAP, BLOCK), BF16),
-            pltpu.VMEM((COLS - 1, SNAP, COLS * SNAP), F32),
-            pltpu.VMEM((COLS - 1, SNAP, COLS * SNAP), F32),
+            pltpu.VMEM((COLS, SNAP, COLS * SNAP), F32),
+            pltpu.VMEM((2, COLS, SNAP, COLS * SNAP), F32),
             pltpu.VMEM((8, SNAP, COLS * SNAP), F32),
-            pltpu.VMEM((8, SNAP, COLS * SNAP), F32),
+            pltpu.VMEM((4, SNAP, COLS * SNAP), F32),
             dma((OWN,)),
             dma((4,)),
             dma((2,)),
             dma((2,)),
         ]
-        + [dma((7,))] * 10,
+        + [dma((7,))] * 4
+        + [dma((2, COLS))] * 2
+        + [dma((7,))] * 4,
         compiler_params=pltpu.CompilerParams(
             collective_id=0, has_side_effects=True, vmem_limit_bytes=32 * 2**20
         ),

time: 42.9 us -> 42.6 us (level); the launches traced: 42.7 us -> 42 us
  Pallas kernels: 40.8 us -> 40.1 us
    pallas_call x1, Pallas kernels: 40.8 us -> 40.1 us  [body(): pl.pallas_call(kernel, out_shape=(jax.ShapeDtypeStruct((3, SNAP, NODES),...]
where the time goes in v4:
time: 42.6 us; the launch traced here: 42 us
  Pallas kernels  40.1 us (94%)
  local copies, waits for them, and re-layouts  1.28 us (3%)
  between operations  0.64 us (2%)
    pallas_call x1, Pallas kernels, body(): pl.pallas_call(kernel, out_shape=(jax.ShapeDtypeStruct((3, SNAP, NODES),...  40.1 us
    unnamed x2, local copies, waits for them, and re-layouts  1.28 us

profile of v4, /device:TPU:1, one launch (start us, length us, event | category | flops | bytes accessed | tf_op | source)
XLA Modules:
  0.0 42.0 jit_solution(9330378880543938132)
XLA Ops:
  0.6 40.1 %shard_map.68 = (bf16[3,16,2048]{2,1,0:T(8,128)(2,1)S(1)}, f32[16,128]{1,0:T(8,128)S(1)}) custom-call(bf16[3,16,2048]{2,1,0:T(8,128)(2,1)} %bitcast.9, bf16[3,3,16,2048]{3,2,1,0:T(8,128)(2,1)} %bitcast.8, s32[15,2048]{1,0:T(8,128)} %slot_hbm.1, s32[1,512]{1,0:T(1,128)} %bitcast.10, s32[1,512]{1,0:T(1,128)} %bitcast.11), custom_call_target="tpu_custom_call" | custom-call | flops 9100000256 | bytes 1200000 | tf_op jit(solution)/shard_map/pallas_call | solution.py:344
  40.7 0.7 %copy.9 = bf16[16,3,2048]{2,0,1:T(8,128)(2,1)} copy(bf16[16,3,2048]{2,0,1:T(8,128)(2,1)S(1)} %bitcast.6) | data formatting | bytes 393216
  41.4 0.6 %copy.10 = f32[128,16]{0,1:T(8,128)} copy(f32[128,16]{0,1:T(8,128)S(1)} %bitcast.7) | data formatting | bytes 16384

commit v5 on v4

--- a/solution.py
+++ b/solution.py
@@ -260,7 +260,7 @@
         total = products(first, last + 1 if also_own else last)
         for step in range(first, last):
             part_out[step] = total[(step - first) * SNAP : (step - first + 1) * SNAP]
-            for side in range(2):
+            for side in (1, 0):
                 part_copy(step, side, core).start()
         return total[(last - first) * SNAP :]
 
@@ -321,9 +321,9 @@
             total = total + slots[other]
         return total, copies
 
-    z_sum, z_copies = exchange(chip_part, z_pos, z_in, FAR_FIRST, z_peer, z_send, z_recv)
-    x_sum, x_copies = exchange(z_sum, x_pos, x_in, X_STEPS, x_peer, x_send, x_recv)
-    gram_ref[...] = x_sum / (3.0 * NODES * 64)
+    x_sum, x_copies = exchange(chip_part, x_pos, x_in, X_STEPS, x_peer, x_send, x_recv)
+    z_sum, z_copies = exchange(x_sum, z_pos, z_in, FAR_FIRST, z_peer, z_send, z_recv)
+    gram_ref[...] = z_sum / (3.0 * NODES * 64)
 
     for copy in z_copies + x_copies:
         copy.wait_send()

time: 42.6 us -> 42.6 us (level)
  the two profiles are of different devices: /device:TPU:1 before, /device:TPU:16 now
where the time goes in v5:
time: 42.6 us; the launch traced here: 42.4 us
  Pallas kernels  40.5 us (95%)
  local copies, waits for them, and re-layouts  1.28 us (3%)
  between operations  0.64 us (2%)
    pallas_call x1, Pallas kernels, body(): pl.pallas_call(kernel, out_shape=(jax.ShapeDtypeStruct((3, SNAP, NODES),...  40.5 us
    unnamed x2, local copies, waits for them, and re-layouts  1.28 us

profile of v5, /device:TPU:16, one launch (start us, length us, event | category | flops | bytes accessed | tf_op | source)
XLA Modules:
  0.0 42.4 jit_solution(6296065687255092256)
XLA Ops:
  0.6 40.5 %shard_map.68 = (bf16[3,16,2048]{2,1,0:T(8,128)(2,1)S(1)}, f32[16,128]{1,0:T(8,128)S(1)}) custom-call(bf16[3,16,2048]{2,1,0:T(8,128)(2,1)} %bitcast.9, bf16[3,3,16,2048]{3,2,1,0:T(8,128)(2,1)} %bitcast.8, s32[15,2048]{1,0:T(8,128)} %slot_hbm.1, s32[1,512]{1,0:T(1,128)} %bitcast.10, s32[1,512]{1,0:T(1,128)} %bitcast.11), custom_call_target="tpu_custom_call" | custom-call | flops 9100000256 | bytes 1200000 | tf_op jit(solution)/shard_map/pallas_call | solution.py:344
  41.2 0.7 %copy.9 = bf16[16,3,2048]{2,0,1:T(8,128)(2,1)} copy(bf16[16,3,2048]{2,0,1:T(8,128)(2,1)S(1)} %bitcast.6) | data formatting | bytes 393216
  41.8 0.6 %copy.10 = f32[128,16]{0,1:T(8,128)} copy(f32[128,16]{0,1:T(8,128)S(1)} %bitcast.7) | data formatting | bytes 16384
